TPU v7x, 32 devices: a whole 2x2x4 slice. The times are simulated.
32 devices in a mesh: grp: 4 (over z), mem: 8 (over y, x, core).
Axes of the slice: x: 2, y: 2, z: 4, core: 2. Of those that a mesh axis runs over, the one named last changes fastest.
Arguments:
- spectra: bfloat16 [128, 8, 2, 1024], P(('grp', 'mem')), may hold values from -6 to 6
- seg_mask: int32 [128, 8], P(('grp', 'mem')), may hold values 0 or 1
- chan_pos: int32 [128], P(('grp', 'mem')), may hold values from 0 to 127, each once
Outputs:
- correlations: bfloat16 [128, 4, 32, 128], P('grp', None, 'mem')
Inputs may be any that keep to these rules, and one draw needn't show every extreme that they name: `seg_mask`: segment validity is 0 or 1. `chan_pos`: each position appears once.
All inputs are finite; a program needn't handle non-finite values. No bound on the sum of `seg_mask` on one device may be relied on, other than what follows from the above.
Results may differ from a plain program's by a relative error of at most 0.0045.
Values may be sent and summed in bfloat16 or wider, within the bound.
A program may use at most 128 MiB of HBM per device.

v0:
```python
import math
import jax
import jax.numpy as jnp
from jax import lax
from jax.sharding import PartitionSpec as P

BINS = 1024
LAGS = 128


def make_table(bins, lags):
    freq = jnp.arange(bins, dtype=jnp.int32)
    lag_ids = jnp.arange(lags, dtype=jnp.int32) - lags // 2
    phase = jnp.mod(freq[:, None] * lag_ids[None, :], bins).astype(jnp.float32) * (
        2.0 * math.pi / bins
    )
    table = jnp.concatenate([jnp.cos(phase), -jnp.sin(phase)], axis=0).astype(jnp.bfloat16)
    return (table, lag_ids.astype(jnp.float32))


def pick_block(count, most):
    best = 1
    for candidate in range(1, count + 1):
        if count % candidate == 0 and candidate <= most:
            best = candidate
    return best


def correlate(rows, cols, table, lag_vals, ratio, scale):
    row_spec, row_ints = rows
    col_spec, col_ints = cols
    nrows = row_spec.shape[0]
    ncols = col_spec.shape[0]
    segs = col_spec.shape[1]
    bins = col_spec.shape[3]
    lags = table.shape[1]
    col_flat = col_spec.reshape(ncols, 2 * segs, bins)
    turned = jnp.stack((-col_spec[:, :, 1], col_spec[:, :, 0]), axis=2).reshape(
        ncols, 2 * segs, bins
    )
    bstack = jnp.stack([col_flat, turned], axis=1)
    col_mask = col_ints[:, :segs].astype(jnp.float32)
    col_pos = col_ints[:, segs].astype(jnp.float32)
    block = pick_block(nrows, max(1, 1024 // ncols))

    def one_block(args):
        spec_blk, int_blk = args
        cross = jnp.einsum(
            "itf,jctf->ijcf", spec_blk, bstack, preferred_element_type=jnp.float32
        ).astype(jnp.bfloat16)
        raw = jnp.dot(
            cross.reshape(block * ncols, 2 * bins), table, preferred_element_type=jnp.float32
        ).reshape(block, ncols, lags)
        count = jnp.dot(
            int_blk[:, :segs].astype(jnp.float32), col_mask.T, precision=lax.Precision.HIGHEST
        )
        dist = jnp.abs(int_blk[:, segs].astype(jnp.float32)[:, None] - col_pos[None, :])
        span = 1.0 + dist * ratio
        taper = 1.0 / (1.0 + (lag_vals / span[:, :, None]) ** 2)
        norm = 1.0 / (scale * jnp.maximum(count, 1.0))
        return (raw * taper * norm[:, :, None]).astype(jnp.bfloat16)

    spec_rows = row_spec.reshape(nrows // block, block, 2 * segs, bins)
    int_rows = row_ints.reshape(nrows // block, block, row_ints.shape[1])
    out = lax.map(one_block, (spec_rows, int_rows))
    return out.reshape(nrows, ncols, lags)


def body(spectra, seg_mask, chan_pos):
    masked = spectra * seg_mask.astype(jnp.bfloat16)[:, :, None, None]
    ints = jnp.concatenate([seg_mask, chan_pos[:, None]], axis=1)
    chans = spectra.shape[0] * lax.axis_size("grp") * lax.axis_size("mem")
    table, lag_vals = make_table(BINS, LAGS)
    ratio = LAGS / chans
    scale = math.sqrt(BINS)
    cols = (
        lax.all_gather(masked, "grp", axis=0, tiled=True),
        lax.all_gather(ints, "grp", axis=0, tiled=True),
    )
    result = correlate(
        lax.all_gather((masked, ints), "mem", axis=0, tiled=True),
        cols,
        table,
        lag_vals,
        ratio,
        scale,
    )
    return result.reshape(result.shape[0], lax.axis_size("grp"), spectra.shape[0], LAGS)


def solution(mesh):
    in_specs = (P(("grp", "mem"), None, None, None), P(("grp", "mem"), None), P(("grp", "mem")))
    out_specs = P("grp", None, "mem", None)
    return jax.shard_map(body, mesh=mesh, in_specs=in_specs, out_specs=out_specs, check_vma=False)
```

profile of v0, /device:TPU:0, one launch (start us, length us, event | category | flops | bytes accessed | tf_op | source)
XLA Modules:
  0.0 105.4 jit_solution(3508888565890975375)
XLA Ops:
  6.5 0.7 convert_element_type.51
  7.2 1.6 %copy_multiply_fusion = bf16[4,8,2,1024]{3,1,2,0:T(8,128)(2,1)} fusion(bf16[4,8,2,1024]{3,2,1,0:T(2,128)(2,1)} %param.3, bf16[4,8]{1,0:T(4,128)(2,1)S(1)} %convert_element_type.51), kind=kLoop, calls=%fused_computation.30 | loop fusion | flops 65536 | bytes 262208 | tf_op jit(solution)/shard_map/mul | solution.py:70
  8.9 17.6 %all_gather.12 = bf16[16,8,2,1024]{3,1,2,0:T(8,128)(2,1)S(1)} all-gather(bf16[4,8,2,1024]{3,1,2,0:T(8,128)(2,1)} %copy_multiply_fusion), channel_id=1, replica_groups=mesh['grp'=4,'mem'=8] {'grp'}, dimensions={0}, use_global_device_ids=true | all-gather | bytes 655360 | tf_op jit(solution)/shard_map/all_gather | solution.py:77
  26.5 0.3 copy.38
  26.9 4.9 %copy.42 = bf16[16,1,16,1024]{2,0,1,3:T(8,128)(2,1)} copy(bf16[16,1,16,1024]{3,0,2,1:T(8,128)(2,1)S(1)} %bitcast.24) | data formatting | bytes 1048576 | tf_op jit(solution)/shard_map/stack;reshape | solution.py:41
  31.8 4.9 %copy.41 = bf16[16,1,16,1024]{2,0,1,3:T(8,128)(2,1)} copy(bf16[16,1,16,1024]{3,0,2,1:T(8,128)(2,1)S(1)} %bitcast.22) | data formatting | bytes 1048576 | tf_op jit(solution)/shard_map/stack;reshape | solution.py:41
  36.7 0.1 copy.45
  36.8 0.1 add_bitcast_fusion
  36.9 8.9 %all-gather = s32[8,4,9]{2,1,0:T(4,128)S(1)} all-gather(s32[1,4,9]{2,1,0:T(4,128)S(1)} %add_bitcast_fusion), channel_id=1, replica_groups=mesh['grp'=4,'mem'=8] {'mem'}, dimensions={0}, use_global_device_ids=true | all-gather | bytes 1296 | tf_op jit(solution)/shard_map/all_gather | solution.py:81
  45.8 0.1 slice_convert_fusion.2
  45.8 0.1 copy.53
  45.9 12.2 %all-gather.1 = s32[4,4,9]{2,1,0:T(4,128)S(1)} all-gather(s32[1,4,9]{2,1,0:T(4,128)S(1)} %add_bitcast_fusion), channel_id=1, replica_groups=mesh['grp'=4,'mem'=8] {'grp'}, dimensions={0}, use_global_device_ids=true | all-gather | bytes 720 | tf_op jit(solution)/shard_map/all_gather | solution.py:78
  58.1 0.1 slice_convert_fusion.5
  58.1 0.1 copy.54
  58.2 0.1 abs_add_fusion
  58.3 0.1 copy.48
  58.4 0.2 fusion.9
  58.5 0.1 copy.49
  58.6 2.2 %cosine_convert_fusion = (bf16[1024,128]{1,0:T(8,128)(2,1)S(1)}, bf16[1024,128]{1,0:T(8,128)(2,1)S(1)}) fusion(s32[128]{0:T(128)S(1)} %iota_add_fusion), kind=kLoop, calls=%fused_computation.22 | loop fusion | flops 2228224 | bytes 524800 | tf_op jit(solution)/shard_map/convert
  60.9 7.7 %copy.43 = bf16[32,8,2,1024]{0,2,1,3:T(2,128)(2,1)} copy(bf16[32,8,2,1024]{3,1,2,0:T(8,128)(2,1)} %all-gather.4.cloned.1.call-done) | data formatting | bytes 2097152 | tf_op jit(solution)/shard_map/all_gather | solution.py:81
  68.6 10.2 %convert_bitcast_fusion = bf16[32,16,2,1024]{0,1,2,3:T(8,128)(2,1)} fusion(bf16[32,16,1024,1]{0,1,3,2:T(8,128)(2,1)} %bitcast.23, bf16[16,1,16,1024]{2,0,1,3:T(8,128)(2,1)} %copy.42, bf16[16,1,16,1024]{2,0,1,3:T(8,128)(2,1)} %copy.41), kind=kOutput, calls=%fused_computation.4 | convolution fusion | flops 35127296 | bytes 4194304 | tf_op jit(solution)/shard_map/while/body/eval_jaxpr/itf,jctf->ijcf/dot_general | solution.py:48
  78.8 14.0 %copy.44 = bf16[32,16,2,1024]{3,2,1,0:T(2,128)(2,1)S(1)} copy(bf16[32,16,2,1024]{0,1,2,3:T(8,128)(2,1)} %convert_bitcast_fusion) | data formatting | bytes 4194304 | tf_op jit(solution)/shard_map/while/body/eval_jaxpr/convert_element_type | solution.py:50
  92.8 2.8 %dot_general.15 = bf16[32,16,2048]{2,1,0:T(8,128)(2,1)} reshape(bf16[32,16,2,1024]{3,2,1,0:T(2,128)(2,1)S(1)} %copy.44) | data formatting | bytes 4194304 | tf_op jit(solution)/shard_map/while/body/eval_jaxpr/dot_general | solution.py:51
  95.6 3.0 %fusion.7 = bf16[32,16,128]{2,1,0:T(8,128)(2,1)} fusion(bf16[32,16,2048]{2,1,0:T(8,128)(2,1)} %dot_general.15, bf16[1024,128]{1,0:T(8,128)(2,1)S(1)} %get-tuple-element.24, bf16[1024,128]{1,0:T(8,128)(2,1)S(1)} %get-tuple-element.23, f32[32,16]{1,0:T(8,128)S(1)} %copy.49, f32[32,16]{1,0:T(8,128)S(1)} %copy.48, f32[128]{0:T(128)S(1)} %fusion.20), kind=kOutput, calls=%fused_computation.7 | convolution fusion | flops 269942784 | bytes 2757120 | tf_op jit(solution)/shard_map/while/body/eval_jaxpr/dot_general | solution.py:51
  (11 shorter events, 0.1 us)
Async XLA Ops:
  6.5 54.4 %all-gather.4.cloned.1.call-start = ((), (), s32[]{:S(2)}) async-start(), calls=%async_computation | async-start | bytes 1179648 | tf_op jit(solution)/shard_map/all_gather | solution.py:81
  26.9 9.8 %copy-start.1 = (s32[4]{0:T(128)S(1)}, s32[4]{0:T(128)}, u32[]{:S(2)}) copy-start(s32[4]{0:T(128)} %param.5) | copy-start | bytes 52
  26.9 9.9 %copy-start = (s32[4,8]{1,0:T(4,128)S(1)}, s32[4,8]{1,0:T(4,128)}, u32[]{:S(2)}) copy-start(s32[4,8]{1,0:T(4,128)} %param.4) | copy-start | bytes 388
Sparse Core Ops, SparseCore 0:
  9.2 26.1 all-gather.3
where the time goes:
time: 106 us; the launch traced here: 105 us
  blocking collectives  38.6 us (36%)
  local copies, waits for them, and re-layouts  35 us (33%)
  between operations  13.5 us (13%)
  matrix products  13.3 us (13%)
  other arithmetic  4.95 us (5%)
    all_gather x1, blocking collectives, body(): lax.all_gather(masked, 'grp', axis=0, tiled=True)  17.6 us
    convert_element_type x1, local copies, waits for them, and re-layouts, one_block(): cross = jnp.einsum('itf,jctf->ijcf', spec_blk, bstack, preferred_element_...  14 us
    all_gather x1, blocking collectives, body(): lax.all_gather(ints, 'grp', axis=0, tiled=True)  12.2 us
    dot_general x1, matrix products, one_block(): jnp.einsum('itf,jctf->ijcf', spec_blk, bstack, preferred_element_type=jnp...  10.2 us
    another operation x2, local copies, waits for them, and re-layouts, correlate(): bstack = jnp.stack([col_flat, turned], axis=1)  9.81 us
    all_gather x1, blocking collectives, body(): lax.all_gather((masked, ints), 'mem', axis=0, tiled=True)  8.89 us
    all_gather x1, local copies, waits for them, and re-layouts, body(): lax.all_gather((masked, ints), 'mem', axis=0, tiled=True)  7.69 us
    dot_general x1, matrix products, one_block(): jnp.dot(cross.reshape(block * ncols, 2 * bins), table, preferred_element_...  2.96 us
  transfers between devices with their start and end apart: 1, of which 0 were waited for; matrix products, arithmetic and copies ran while one was open for 13% of the time, Pallas kernels for 0%

commit v1 on v0

--- a/solution.py
+++ b/solution.py
@@ -6,6 +6,19 @@
 
 BINS = 1024
 LAGS = 128
+
+
+def gather_around(array, axis, dim):
+    ways = lax.axis_size(axis)
+    up = [(d, (d + 1) % ways) for d in range(ways)]
+    down = [(d, (d - 1) % ways) for d in range(ways)]
+    earlier, later = ([array], [array])
+    for _ in range(ways // 2):
+        earlier.append(lax.ppermute(earlier[-1], axis, up))
+    for _ in range((ways - 1) // 2):
+        later.append(lax.ppermute(later[-1], axis, down))
+    line = jnp.concatenate([*earlier[::-1], *later[1:]], axis=dim)
+    return jnp.roll(line, (lax.axis_index(axis) - ways // 2) * array.shape[dim], axis=dim)
 
 
 def make_table(bins, lags):
@@ -73,10 +86,7 @@
     table, lag_vals = make_table(BINS, LAGS)
     ratio = LAGS / chans
     scale = math.sqrt(BINS)
-    cols = (
-        lax.all_gather(masked, "grp", axis=0, tiled=True),
-        lax.all_gather(ints, "grp", axis=0, tiled=True),
-    )
+    cols = (gather_around(masked, "grp", 0), lax.all_gather(ints, "grp", axis=0, tiled=True))
     result = correlate(
         lax.all_gather((masked, ints), "mem", axis=0, tiled=True),
         cols,

time: 106 us -> 103 us (0.972)
  blocking collectives: 38.6 us -> 20.9 us
  waiting for transfers between devices: 0.04 us -> 6.54 us
  starting transfers between devices: 0.01 us -> 5.23 us
  local copies, waits for them, and re-layouts: 35 us -> 37.2 us
    all_gather x1 -> x0, blocking collectives: 17.6 us -> none  [body(): lax.all_gather(masked, 'grp', axis=0, tiled=True)]
    ppermute x0 -> x3, waiting for transfers between devices: none -> 6.52 us  [the longest x2 6.52 us: gather_around(): earlier.append(lax.ppermute(earlier[-1], axis, up))]
    ppermute x0 -> x3, starting transfers between devices: none -> 5.23 us  [the longest x2 3.13 us: gather_around(): earlier.append(lax.ppermute(earlier[-1], axis, up))]
  transfers between devices with their start and end apart: 1 -> 4, of which waited for: 0 -> 1; matrix products, arithmetic and copies ran while one was open for 13% -> 16% of each run, Pallas kernels for 0% -> 0%
where the time goes in v1:
time: 103 us; the launch traced here: 102 us
  local copies, waits for them, and re-layouts  37.2 us (36%)
  blocking collectives  20.9 us (20%)
  between operations  13.5 us (13%)
  matrix products  13.3 us (13%)
  waiting for transfers between devices  6.54 us (6%)
  starting transfers between devices  5.23 us (5%)
  other arithmetic  5.18 us (5%)
    convert_element_type x1, local copies, waits for them, and re-layouts, one_block(): cross = jnp.einsum('itf,jctf->ijcf', spec_blk, bstack, preferred_element_...  14 us
    all_gather x1, blocking collectives, body(): lax.all_gather(ints, 'grp', axis=0, tiled=True)  11.9 us
    dot_general x1, matrix products, one_block(): jnp.einsum('itf,jctf->ijcf', spec_blk, bstack, preferred_element_type=jnp...  10.2 us
    another operation x2, local copies, waits for them, and re-layouts, correlate(): bstack = jnp.stack([col_flat, turned], axis=1)  9.8 us
    all_gather x1, blocking collectives, body(): lax.all_gather((masked, ints), 'mem', axis=0, tiled=True)  9.05 us
    all_gather x1, local copies, waits for them, and re-layouts, body(): lax.all_gather((masked, ints), 'mem', axis=0, tiled=True)  7.68 us
    ppermute x2, waiting for transfers between devices, gather_around(): earlier.append(lax.ppermute(earlier[-1], axis, up))  6.52 us
    ppermute x2, starting transfers between devices, gather_around(): earlier.append(lax.ppermute(earlier[-1], axis, up))  3.13 us
  transfers between devices with their start and end apart: 4, of which 1 were waited for; matrix products, arithmetic and copies ran while one was open for 16% of the time, Pallas kernels for 0%

profile of v1, /device:TPU:0, one launch (start us, length us, event | category | flops | bytes accessed | tf_op | source)
XLA Modules:
  0.0 101.9 jit_solution(4156174885810586245)
XLA Ops:
  6.5 0.7 convert_element_type.51
  7.2 0.1 copy.36
  7.3 1.0 %copy_multiply_fusion = bf16[4,8,2,1024]{3,0,2,1:T(4,128)(2,1)S(1)} fusion(bf16[4,8,2,1024]{3,2,1,0:T(2,128)(2,1)} %param.3, bf16[4,8]{0,1:T(8,128)(2,1)S(1)} %copy.36), kind=kLoop, calls=%fused_computation.30 | loop fusion | flops 65536 | bytes 262208 | tf_op jit(solution)/shard_map/mul | solution.py:83
  8.3 3.1 %collective-permute-start = (bf16[4,8,2,1024]{3,0,2,1:T(4,128)(2,1)S(1)}, bf16[4,8,2,1024]{3,0,2,1:T(4,128)(2,1)S(1)}, u32[]{:S(2)}, u32[]{:S(2)}) collective-permute-start(bf16[4,8,2,1024]{3,0,2,1:T(4,128)(2,1)S(1)} %copy_multiply_fusion), channel_id=1, source_target_pairs={{0,8},{8,16},{16,24},{24,0},{1,9},{9,17},{17,25},{25,1},{2,10},{10... | collective-permute-start | bytes 393224 | tf_op jit(solution)/shard_map/ppermute | solution.py:17
  11.4 2.1 %collective-permute-start.2 = (bf16[4,8,2,1024]{3,0,2,1:T(4,128)(2,1)S(1)}, bf16[4,8,2,1024]{3,0,2,1:T(4,128)(2,1)S(1)}, u32[]{:S(2)}, u32[]{:S(2)}) collective-permute-start(bf16[4,8,2,1024]{3,0,2,1:T(4,128)(2,1)S(1)} %copy_multiply_fusion), channel_id=1, source_target_pairs={{0,24},{8,0},{16,8},{24,16},{1,25},{9,1},{17,9},{25,17},{2,26},{10... | collective-permute-start | bytes 393224 | tf_op jit(solution)/shard_map/ppermute | solution.py:19
  13.5 0.7 copy.40
  14.3 0.7 copy.43
  15.0 0.8 add_bitcast_fusion
  15.8 9.0 %all-gather = s32[8,4,9]{2,1,0:T(4,128)S(1)} all-gather(s32[1,4,9]{2,1,0:T(4,128)S(1)} %add_bitcast_fusion), channel_id=1, replica_groups=mesh['grp'=4,'mem'=8] {'mem'}, dimensions={0}, use_global_device_ids=true | all-gather | bytes 1296 | tf_op jit(solution)/shard_map/all_gather | solution.py:91
  25.0 11.9 %all-gather.1 = s32[4,4,9]{2,1,0:T(4,128)S(1)} all-gather(s32[1,4,9]{2,1,0:T(4,128)S(1)} %add_bitcast_fusion), channel_id=1, replica_groups=mesh['grp'=4,'mem'=8] {'grp'}, dimensions={0}, use_global_device_ids=true | all-gather | bytes 720 | tf_op jit(solution)/shard_map/all_gather | solution.py:89
  36.9 0.1 copy.52
  37.0 2.2 %cosine_convert_fusion = (bf16[1024,128]{1,0:T(8,128)(2,1)S(1)}, bf16[1024,128]{1,0:T(8,128)(2,1)S(1)}) fusion(s32[128]{0:T(128)S(1)} %iota_add_fusion), kind=kLoop, calls=%fused_computation.22 | loop fusion | flops 2228224 | bytes 524800 | tf_op jit(solution)/shard_map/convert
  39.2 0.1 fusion.9
  39.7 6.5 %collective-permute-done.1 = bf16[4,8,2,1024]{3,0,2,1:T(4,128)(2,1)S(1)} collective-permute-done((bf16[4,8,2,1024]{3,0,2,1:T(4,128)(2,1)S(1)}, bf16[4,8,2,1024]{3,0,2,1:T(4,128)(2,1)S(1)}, u32[]{:S(2)}, u32[]{:S(2)}) %collective-permute-start.1) | collective-permute-done | bytes 131104 | tf_op jit(solution)/shard_map/ppermute | solution.py:17
  46.2 0.9 concatenate.13
  47.1 0.2 dynamic-slice_negate_fusion
  47.4 4.9 %copy.39 = bf16[16,1,16,1024]{2,0,1,3:T(8,128)(2,1)} copy(bf16[16,1,16,1024]{3,0,2,1:T(8,128)(2,1)S(1)} %bitcast.23) | data formatting | bytes 1048576 | tf_op jit(solution)/shard_map/stack;reshape | solution.py:54
  52.3 0.2 constant_dynamic-slice_fusion.1
  52.5 4.9 %copy.38 = bf16[16,1,16,1024]{2,0,1,3:T(8,128)(2,1)} copy(bf16[16,1,16,1024]{3,0,2,1:T(8,128)(2,1)S(1)} %bitcast.24) | data formatting | bytes 1048576 | tf_op jit(solution)/shard_map/stack;reshape | solution.py:54
  57.4 7.7 %copy.41 = bf16[32,8,2,1024]{0,2,1,3:T(2,128)(2,1)} copy(bf16[32,8,2,1024]{3,1,2,0:T(8,128)(2,1)} %all-gather.4.cloned.1.call-done) | data formatting | bytes 2097152 | tf_op jit(solution)/shard_map/all_gather | solution.py:91
  65.1 10.2 %convert_bitcast_fusion = bf16[32,16,2,1024]{0,1,2,3:T(8,128)(2,1)} fusion(bf16[32,16,1024,1]{0,1,3,2:T(8,128)(2,1)} %bitcast.22, bf16[16,1,16,1024]{2,0,1,3:T(8,128)(2,1)} %copy.39, bf16[16,1,16,1024]{2,0,1,3:T(8,128)(2,1)} %copy.38), kind=kOutput, calls=%fused_computation.4 | convolution fusion | flops 35127296 | bytes 4194304 | tf_op jit(solution)/shard_map/while/body/eval_jaxpr/itf,jctf->ijcf/dot_general | solution.py:61
  75.3 14.0 %copy.42 = bf16[32,16,2,1024]{3,2,1,0:T(2,128)(2,1)S(1)} copy(bf16[32,16,2,1024]{0,1,2,3:T(8,128)(2,1)} %convert_bitcast_fusion) | data formatting | bytes 4194304 | tf_op jit(solution)/shard_map/while/body/eval_jaxpr/convert_element_type | solution.py:63
  89.3 2.8 %dot_general.15 = bf16[32,16,2048]{2,1,0:T(8,128)(2,1)} reshape(bf16[32,16,2,1024]{3,2,1,0:T(2,128)(2,1)S(1)} %copy.42) | data formatting | bytes 4194304 | tf_op jit(solution)/shard_map/while/body/eval_jaxpr/dot_general | solution.py:64
  92.1 3.0 %fusion.7 = bf16[32,16,128]{2,1,0:T(8,128)(2,1)} fusion(bf16[32,16,2048]{2,1,0:T(8,128)(2,1)} %dot_general.15, bf16[1024,128]{1,0:T(8,128)(2,1)S(1)} %get-tuple-element.24, bf16[1024,128]{1,0:T(8,128)(2,1)S(1)} %get-tuple-element.23, f32[32,16]{1,0:T(8,128)S(1)} %copy.47, f32[32,16]{1,0:T(8,128)S(1)} %copy.46, f32[128]{0:T(128)S(1)} %fusion.20), kind=kOutput, calls=%fused_computation.7 | convolution fusion | flops 269942784 | bytes 2757120 | tf_op jit(solution)/shard_map/while/body/eval_jaxpr/dot_general | solution.py:64
  (15 shorter events, 0.6 us)
Async XLA Ops:
  6.5 50.9 %all-gather.4.cloned.1.call-start = ((), (), s32[]{:S(2)}) async-start(), calls=%async_computation | async-start | bytes 1179648 | tf_op jit(solution)/shard_map/all_gather | solution.py:91
  8.3 31.0 %collective-permute-start = (bf16[4,8,2,1024]{3,0,2,1:T(4,128)(2,1)S(1)}, bf16[4,8,2,1024]{3,0,2,1:T(4,128)(2,1)S(1)}, u32[]{:S(2)}, u32[]{:S(2)}) collective-permute-start(bf16[4,8,2,1024]{3,0,2,1:T(4,128)(2,1)S(1)} %copy_multiply_fusion), channel_id=1, source_target_pairs={{0,8},{8,16},{16,24},{24,0},{1,9},{9,17},{17,25},{25,1},{2,10},{10... | collective-permute-start | bytes 393224 | tf_op jit(solution)/shard_map/ppermute | solution.py:17
  11.4 28.3 %collective-permute-start.2 = (bf16[4,8,2,1024]{3,0,2,1:T(4,128)(2,1)S(1)}, bf16[4,8,2,1024]{3,0,2,1:T(4,128)(2,1)S(1)}, u32[]{:S(2)}, u32[]{:S(2)}) collective-permute-start(bf16[4,8,2,1024]{3,0,2,1:T(4,128)(2,1)S(1)} %copy_multiply_fusion), channel_id=1, source_target_pairs={{0,24},{8,0},{16,8},{24,16},{1,25},{9,1},{17,9},{25,17},{2,26},{10... | collective-permute-start | bytes 393224 | tf_op jit(solution)/shard_map/ppermute | solution.py:19
  39.4 6.8 %collective-permute-start.1 = (bf16[4,8,2,1024]{3,0,2,1:T(4,128)(2,1)S(1)}, bf16[4,8,2,1024]{3,0,2,1:T(4,128)(2,1)S(1)}, u32[]{:S(2)}, u32[]{:S(2)}) collective-permute-start(bf16[4,8,2,1024]{3,0,2,1:T(4,128)(2,1)S(1)} %collective-permute-done), channel_id=1, source_target_pairs={{0,8},{8,16},{16,24},{24,0},{1,9},{9,17},{17,25},{25,1},{2,10},{10... | collective-permute-start | bytes 393224 | tf_op jit(solution)/shard_map/ppermute | solution.py:17
Sparse Core Ops, SparseCore 0:
  14.4 23.0 all-gather.3
